TPU v7x, 256 devices: a whole 4x4x8 slice. The times are simulated.
256 devices in a mesh: ctx: 64 (over y_lo, x, z), head: 4 (over y_hi, core).
Axes of the slice: x: 4, y: 4 (y_hi: 2, y_lo: 2; y = y_hi * 2 + y_lo), z: 8, core: 2. Of those that a mesh axis runs over, the one named last changes fastest.
Arguments:
- queries: bfloat16 [1, 16384, 2048], P(None, 'ctx', 'head'), may hold values from -128 to 128
- key_rows: bfloat16 [1, 16384, 128], P(None, ('ctx', 'head')), may hold values from -4.5 to 4.5
- value_rows: bfloat16 [1, 16384, 128], P(None, ('ctx', 'head')), may hold values from -5 to 5
- document_lengths: int32 [1, 4], replicated, may hold values from 1 to 12288, 16384 in all within a row
Outputs:
- attended: bfloat16 [1, 16384, 2048], P(None, 'ctx', 'head')
All inputs are finite; a program needn't handle non-finite values.
Results may differ from a plain program's by a relative error of at most 0.0045.
Values may be sent and summed in bfloat16 or wider, within the bound.
A program may use at most 64 MiB of HBM per device.

v0:
```python
import math

import jax
import jax.numpy as jnp
from jax import lax
from jax.sharding import PartitionSpec as P

NEG = -1e30


def document_ids(positions, ends):
    return jnp.sum((positions[None, :, None] >= ends[:, None, :]).astype(jnp.int32), axis=2)


def body(queries, key_rows, value_rows, document_lengths):
    device = lax.axis_index("ctx")
    seqs, rows, width = queries.shape
    head_size = key_rows.shape[2]
    heads = width // head_size
    scale = 1.0 / math.sqrt(head_size)
    ends = jnp.cumsum(document_lengths, axis=1)
    query_pos = device * rows + jnp.arange(rows, dtype=jnp.int32)
    query_docs = document_ids(query_pos, ends)
    query_heads = queries.reshape(seqs, rows, heads, head_size)

    def update(state, key_block, value_block, valid):
        running_max, running_total, accum = state
        scores = (
            jnp.einsum("sqhd,skd->sqhk", query_heads, key_block, preferred_element_type=jnp.float32)
            * scale
        )
        scores = jnp.where(valid[:, :, None, :], scores, NEG)
        new_max = jnp.maximum(running_max, jnp.max(scores, axis=3))
        factor = jnp.exp(running_max - new_max)
        weights = jnp.where(valid[:, :, None, :], jnp.exp(scores - new_max[..., None]), 0.0)
        running_total = running_total * factor + jnp.sum(weights, axis=3)
        accum = accum * factor[..., None] + jnp.einsum(
            "sqhk,skd->sqhd",
            weights.astype(jnp.bfloat16),
            value_block,
            preferred_element_type=jnp.float32,
        )
        return (new_max, running_total, accum)

    initial = (
        jnp.full((seqs, rows, heads), NEG, jnp.float32),
        jnp.zeros((seqs, rows, heads), jnp.float32),
        jnp.zeros((seqs, rows, heads, head_size), jnp.float32),
    )
    key_piece = lax.all_gather(key_rows, ("ctx", "head"), axis=1, tiled=True)
    value_piece = lax.all_gather(value_rows, ("ctx", "head"), axis=1, tiled=True)
    key_count = key_piece.shape[1]
    block_rows = math.gcd(key_count, 256)

    def one_block(block_index, inner):
        offset = block_index * block_rows
        key_block = lax.dynamic_slice_in_dim(key_piece, offset, block_rows, 1)
        value_block = lax.dynamic_slice_in_dim(value_piece, offset, block_rows, 1)
        key_pos = offset + jnp.arange(block_rows, dtype=jnp.int32)
        key_docs = document_ids(key_pos, ends)
        valid = (
            (key_pos[None, None, :] <= query_pos[None, :, None])
            & (key_pos[None, None, :] >= 0)
            & (key_docs[:, None, :] == query_docs[:, :, None])
        )
        return update(inner, key_block, value_block, valid)

    result = lax.fori_loop(0, key_count // block_rows, one_block, initial)
    running_max, running_total, accum = result
    attended = (accum / running_total[..., None]).astype(jnp.bfloat16).reshape(seqs, rows, width)
    return attended


def solution(mesh):
    in_specs = (
        P(None, "ctx", "head"),
        P(None, ("ctx", "head"), None),
        P(None, ("ctx", "head"), None),
        P(),
    )
    out_specs = P(None, "ctx", "head")
    return jax.shard_map(body, mesh=mesh, in_specs=in_specs, out_specs=out_specs, check_vma=False)
```

profile of v0, /device:TPU:1, one launch (start us, length us, event | category | flops | bytes accessed | tf_op | source)
XLA Modules:
  0.0 1045.9 jit_solution(1506735367120556019)
XLA Ops:
  10.2 415.9 %all-gather.3.cloned.1.call-done = bf16[1,16384,128]{2,1,0:T(8,128)(2,1)} async-done(((bf16[1,64,128]{2,1,0:T(8,128)(2,1)}), bf16[1,16384,128]{2,1,0:T(8,128)(2,1)}) %all-gather.3.cloned.1.call-update) | async-done | bytes 4194320 | tf_op jit(solution)/shard_map/all_gather | solution.py:50
  426.2 413.4 %all-gather.5.cloned.1.call-done = bf16[1,16384,128]{2,1,0:T(8,128)(2,1)} async-done(((bf16[1,64,128]{2,1,0:T(8,128)(2,1)}), bf16[1,16384,128]{2,1,0:T(8,128)(2,1)}) %all-gather.5.cloned.1.call-update) | async-done | bytes 4194320 | tf_op jit(solution)/shard_map/all_gather | solution.py:51
  839.6 198.6 %while.18 = (s32[]{:T(128)}, f32[1,256,4]{1,2,0:T(4,128)S(1)}, f32[1,256,4]{1,2,0:T(4,128)S(1)}, f32[1,256,4,128]{3,1,2,0:T(8,128)S(1)}, s32[1,4]{1,0:T(1,128)S(...) while((s32[]{:T(128)}, f32[1,256,4]{1,2,0:T(4,128)S(1)}, ...), condition=%wide.region_6.7_spmd.clone, body=%wide.region_2.6_spmd.clone.sunk | while | flops 137242368 | bytes 4924131 | solution.py:68
  841.1 1.3 fusion.34
  844.2 1.3 fusion.34
  847.3 1.3 fusion.34
  853.5 1.3 fusion.34
  856.6 1.3 fusion.34
  859.7 1.3 fusion.34
  862.8 1.3 fusion.34
  865.9 1.3 fusion.34
  872.1 1.3 fusion.34
  878.3 1.3 fusion.34
  881.4 1.3 fusion.34
  884.5 1.3 fusion.34
  887.6 1.3 fusion.34
  890.7 1.3 fusion.34
  896.9 1.3 fusion.34
  903.1 1.3 fusion.34
  909.4 1.3 fusion.34
  912.5 1.3 fusion.34
  915.6 1.3 fusion.34
  918.7 1.3 fusion.34
  921.8 1.3 fusion.34
  928.0 1.3 fusion.34
  934.2 1.3 fusion.34
  940.4 1.3 fusion.34
  943.5 1.3 fusion.34
  946.6 1.3 fusion.34
  949.7 1.3 fusion.34
  952.8 1.3 fusion.34
  959.0 1.3 fusion.34
  965.2 1.3 fusion.34
  971.4 1.3 fusion.34
  974.5 1.3 fusion.34
  977.6 1.3 fusion.34
  980.7 1.3 fusion.34
  983.8 1.3 fusion.34
  990.0 1.3 fusion.34
  996.2 1.3 fusion.34
  999.3 1.3 fusion.34
  1002.5 1.3 fusion.34
  1005.6 1.3 fusion.34
  1008.7 1.3 fusion.34
  1014.9 1.3 fusion.34
  1021.1 1.3 fusion.34
  1027.3 1.3 fusion.34
  1033.5 1.3 fusion.34
  (608 shorter events, 137.8 us)
Async XLA Ops:
  6.5 419.6 %all-gather.3.cloned.1.call-start = ((), (), s32[]{:S(2)}) async-start(), calls=%async_computation | async-start | bytes 4210688 | tf_op jit(solution)/shard_map/all_gather | solution.py:50
  7.3 832.3 %all-gather.5.cloned.1.call-start = ((), (), s32[]{:S(2)}) async-start(), calls=%async_computation.1 | async-start | bytes 4210688 | tf_op jit(solution)/shard_map/all_gather | solution.py:51
Sparse Core Ops, SparseCore 0:
  9.2 416.8 all-gather.2
  428.0 411.5 all-gather.4
where the time goes:
time: 1050 us
  waiting for transfers between devices  831 us (79%)
  matrix products  161 us (15%)
  other arithmetic  34.4 us (3%)
  between operations  13.5 us (1%)
    all_gather x1, waiting for transfers between devices, body(): key_piece = lax.all_gather(key_rows, ('ctx', 'head'), axis=1, tiled=True)  416 us
    all_gather x1, waiting for transfers between devices, body(): lax.all_gather(value_rows, ('ctx', 'head'), axis=1, tiled=True)  413 us
    dot_general x64, matrix products, update(): jnp.einsum('sqhk,skd->sqhd', weights.astype(jnp.bfloat16), value_block, p...  86.2 us
    dot_general x64, matrix products, update(): jnp.einsum('sqhd,skd->sqhk', query_heads, key_block, preferred_element_ty...  75 us
  transfers between devices with their start and end apart: 2, of which 2 were waited for; matrix products, arithmetic and copies ran while one was open for 0% of the time, Pallas kernels for 0%

commit v1 on v0

v1 whole, which is shorter than its diff:
```python
import functools
import math

import jax
import jax.numpy as jnp
from jax import lax
from jax.experimental import pallas as pl
from jax.experimental.pallas import tpu as pltpu
from jax.sharding import PartitionSpec as P

MESH = pl.DeviceIdType.MESH
HIDE = -(2.0**100)
SCALE = math.log2(math.e) / math.sqrt(128.0)
ROWS = 256
HEADS = 4
WIDE = ROWS * HEADS
KEYS = 256
GROUPS = 8
STEPS = 2 * GROUPS


def device_at(y, x, z, core):
    return ((y % 2) * 32 + x * 8 + z, (y // 2) * 2 + core)


def kernel(
    lengths, q_ref, k_ref, v_ref, o_ref,
    kv, dk, qa, q2, score_a, score_b, acc, top, total, best_a, best_b, o_out, o_in, s_out, s_in,
    y_send, y_recv, x_send, x_recv, vz_send, vz_recv, r_send, r_recv, l_send, l_recv,
    core_send, core_recv, pair_send, pair_recv,
):
    ctx = lax.axis_index("ctx")
    head = lax.axis_index("head")
    y_lo, x, z = ctx // 32, (ctx // 8) % 4, ctx % 8
    y_hi, core = head // 2, head % 2
    y = y_hi * 2 + y_lo
    sibling = device_at(y, x, z, 1 - core)
    partner = device_at(y + 1 - 2 * y_lo, 3 - x, z, core)

    barrier = pltpu.get_barrier_semaphore()
    friends = [
        device_at((y + dy) % 4, x, z, (core + dc) % 2) for dy in range(4) for dc in range(2) if dy + dc > 0
    ]
    friends += [device_at(y, (x + dx) % 4, z, core) for dx in range(1, 4)]
    friends += [device_at(y, x, (z + dz) % 8, core) for dz in range(1, 8)]
    friends += [partner]
    for friend in friends:
        pl.semaphore_signal(barrier, inc=1, device_id=friend, device_id_type=MESH)

    starts, ends, run = [], [], jnp.int32(0)
    for d in range(4):
        starts.append(run)
        run = run + lengths[0, d]
        ends.append(run)

    def fill_queries(which, source):
        late = jnp.where(which == 0, y_lo, 1 - y_lo)
        own_x = jnp.where(which == 0, x, 3 - x)
        block = late * 32 + own_x * 8 + z
        pos = block * ROWS + lax.broadcasted_iota(jnp.int32, (ROWS, 128), 0)
        lane = lax.broadcasted_iota(jnp.int32, (ROWS, 128), 1)
        hide = lane - 64 > block
        for d in range(4):
            inside = (pos >= starts[d]) & (pos < ends[d])
            hide = hide | ((lane == d) & jnp.logical_not(inside))
        extra = jnp.where(hide, HIDE, 0.0).astype(jnp.bfloat16)
        for h in range(HEADS):
            qa[which, h * ROWS : (h + 1) * ROWS, 0:128] = source[:, h * 128 : (h + 1) * 128]
            qa[which, h * ROWS : (h + 1) * ROWS, 128:256] = extra

    def fill_keys(index, carry):
        group, late = index // 2, index % 2
        row = lax.broadcasted_iota(jnp.int32, (512, 128), 0)
        lane = lax.broadcasted_iota(jnp.int32, (512, 128), 1)
        block = late * 32 + (row // 128) * 8 + group
        pos = block * ROWS + ((row // 64) % 2) * 128 + y_lo * 64 + row % 64
        show = lane - 64 == block
        for d in range(4):
            show = show | ((lane == d) & (pos >= starts[d]) & (pos < ends[d]))
        dk[group, late] = jnp.where(show, 1.0, 0.0).astype(jnp.bfloat16)
        return carry

    fill_queries(0, q_ref)
    lax.fori_loop(0, 2 * GROUPS, fill_keys, 0)
    acc[...] = jnp.zeros_like(acc)
    total[...] = jnp.zeros_like(total)
    top[...] = jnp.full_like(top, -1e38)
    pl.semaphore_wait(barrier, len(friends))

    def y_copy(kind, turn):
        rows = kv.at[kind, z, y_lo, pl.ds(x * 128 + y_hi * 64, 64), :]
        return pltpu.make_async_remote_copy(
            src_ref=(k_ref, v_ref)[kind], dst_ref=rows, send_sem=y_send.at[kind, turn], recv_sem=y_recv.at[y],
            device_id=device_at(core + 2 * turn, x, z, kind), device_id_type=MESH,
        )

    def y_stay(kind):
        rows = kv.at[kind, z, y_lo, pl.ds(x * 128 + y_hi * 64, 64), :]
        return pltpu.make_async_copy((k_ref, v_ref)[kind], rows, y_recv.at[y])

    for kind in range(2):
        for turn in range(2):
            here = (core + 2 * turn == y) & (core == kind)
            pl.when(here)(lambda kind=kind: y_stay(kind).start())
            pl.when(jnp.logical_not(here))(lambda kind=kind, turn=turn: y_copy(kind, turn).start())

    pair_q = pltpu.make_async_remote_copy(
        src_ref=q_ref, dst_ref=q2, send_sem=pair_send.at[0], recv_sem=pair_recv.at[0],
        device_id=partner, device_id_type=MESH,
    )
    pair_o = pltpu.make_async_remote_copy(
        src_ref=o_out, dst_ref=o_in, send_sem=pair_send.at[1], recv_sem=pair_recv.at[1],
        device_id=partner, device_id_type=MESH,
    )
    pair_s = pltpu.make_async_remote_copy(
        src_ref=s_out, dst_ref=s_in, send_sem=pair_send.at[2], recv_sem=pair_recv.at[2],
        device_id=partner, device_id_type=MESH,
    )

    def z_of(g):
        far = (g + 1) // 2
        return (z + 8 + jnp.where(g % 2 == 1, -far, far)) % 8

    def column(at_x, at_z):
        return kv.at[core, at_z, :, pl.ds(at_x * 128, 128), :]

    def x_copy(g, dx):
        part = column(x, z_of(g))
        return pltpu.make_async_remote_copy(
            src_ref=part, dst_ref=part, send_sem=x_send.at[g, dx], recv_sem=x_recv.at[g, dx],
            device_id=device_at(y, (x + dx) % 4, z, core), device_id_type=MESH,
        )

    def x_wait(g, dx):
        part = column((x + 4 - dx) % 4, z_of(g))
        pltpu.make_async_copy(part, part, x_recv.at[g, dx]).wait()

    def vz_copy(dz):
        part = column(x, z)
        return pltpu.make_async_remote_copy(
            src_ref=part, dst_ref=part, send_sem=vz_send.at[dz], recv_sem=vz_recv.at[dz],
            device_id=device_at(y, x, (z + dz) % 8, core), device_id_type=MESH,
        )

    def ring_copy(way, hop):
        at = (z + 8 + jnp.where(way == 0, -hop, hop)) % 8
        part = kv.at[0, at] if hop < 3 else kv.at[0, at, way]
        send, recv = ((r_send, r_recv), (l_send, l_recv))[way]
        return pltpu.make_async_remote_copy(
            src_ref=part, dst_ref=part, send_sem=send.at[hop], recv_sem=recv.at[hop],
            device_id=device_at(y, x, (z + (1, 7)[way]) % 8, core), device_id_type=MESH,
        )

    def ring_wait(way, hop):
        at = (z + 8 + jnp.where(way == 0, -hop - 1, hop + 1)) % 8
        part = kv.at[0, at] if hop < 3 else kv.at[0, at, way]
        pltpu.make_async_copy(part, part, (r_recv, l_recv)[way].at[hop]).wait()

    def core_copy(g):
        part = kv.at[core, z_of(g)]
        return pltpu.make_async_remote_copy(
            src_ref=part, dst_ref=part, send_sem=core_send.at[g], recv_sem=core_recv.at[g],
            device_id=sibling, device_id_type=MESH,
        )

    def core_wait(g):
        part = kv.at[1 - core, z_of(g)]
        pltpu.make_async_copy(part, part, core_recv.at[g]).wait()

    def relay_values(g):
        dz = (z + 8 - z_of(g)) % 8
        part = column(x, z_of(g))
        pltpu.make_async_copy(part, part, vz_recv.at[dz]).wait()
        for dx in range(1, 4):
            x_copy(g, dx).start()

    def arrive(g):
        for hop in range(3):
            for way in range(2):

                @pl.when((core == 0) & (g == 2 * hop + 1 + way))
                def _():
                    ring_wait(way, hop)
                    ring_copy(way, hop + 1).start()

        @pl.when((core == 0) & (g == 7))
        def _():
            ring_wait(0, 3)
            ring_wait(1, 3)

        @pl.when(core == 1)
        def _():
            for dx in range(1, 4):
                x_wait(g, dx)

        core_copy(g).start()

        @pl.when((core == 1) & (g == 1))
        def _():
            relay_values(jnp.int32(3))
            relay_values(jnp.int32(4))

        @pl.when((core == 1) & (g == 2))
        def _():
            relay_values(jnp.int32(5))
            relay_values(jnp.int32(6))

        @pl.when((core == 1) & (g == 3))
        def _():
            relay_values(jnp.int32(7))

        core_wait(g)

    zero = jnp.int32(0)
    for yy in range(4):
        rows = kv.at[core, z, yy % 2, pl.ds(x * 128 + (yy // 2) * 64, 64), :]
        pltpu.make_async_copy(k_ref, rows, y_recv.at[yy]).wait()
    for dx in range(1, 4):
        x_copy(zero, dx).start()

    @pl.when(core == 1)
    def _():
        for dz in (1, 7, 2, 6, 3, 5, 4):
            vz_copy(dz).start()

    pair_q.start()
    for dx in range(1, 4):
        x_wait(zero, dx)

    @pl.when(core == 0)
    def _():
        ring_copy(0, 0).start()
        ring_copy(1, 0).start()

    core_copy(zero).start()

    @pl.when(core == 1)
    def _():
        relay_values(jnp.int32(1))
        relay_values(jnp.int32(2))

    core_wait(zero)

    def step_of(i):
        even_set = jnp.where((i >= 4) & (i < 12), 1, 0)
        even_group = jnp.where(i < 4, i, jnp.where(i < 12, i - 4, i - 8))
        odd_set = jnp.where((i < 2) | (i == 5) | (i == 8) | (i >= 12), 0, 1)
        odd_group = jnp.where(
            i < 2, i,
            jnp.where(i < 5, i - 2, jnp.where(i == 5, 2, jnp.where(i < 8, i - 3, jnp.where(i == 8, 3, jnp.where(i < 12, i - 4, i - 8))))),
        )
        which = jnp.where(y_lo == 0, even_set, odd_set)
        g = jnp.where(y_lo == 0, even_group, odd_group)
        return which, g

    def units_of(which, g):
        late = jnp.where(which == 0, y_lo, 1 - y_lo)
        own_x = jnp.where(which == 0, x, 3 - x)
        blocks = own_x + jnp.where(z_of(g) <= z, 1, 0)
        count = (blocks + 1) // 2
        return jnp.where(late == 1, 2 + count, jnp.maximum(count, 1))

    def locate(i, j):
        which, g = step_of(i)
        over = i >= STEPS
        which = jnp.where(over, y_lo, which)
        group = jnp.where(over, z, z_of(g))
        late = jnp.where(over, 1, j // 2)
        row = pl.multiple_of(jnp.where(over, 0, (j % 2) * KEYS), KEYS)
        return which, group, late, row

    def advance(i, j):
        which, g = step_of(i)
        more = (j + 1 < units_of(which, g)) & (i < STEPS)
        return jnp.where(more, i, jnp.minimum(i + 1, STEPS)), jnp.where(more, j + 1, 0)

    def prepare(i, j, got):
        which, g = step_of(i)
        first = (j == 0) & (i < STEPS)
        fresh = first & (g == got)
        pl.when(fresh)(lambda: arrive(g))

        @pl.when(first & (which == 1) & (g == 0))
        def _():
            pair_q.wait_recv()
            fill_queries(1, q2)

        return jnp.where(fresh, got + 1, got)

    def scores_of(i, j, score, best):
        which, group, late, row = locate(i, j)
        keys = jnp.concatenate([kv[0, group, late, pl.ds(row, KEYS), :], dk[group, late, pl.ds(row, KEYS), :]], axis=1)
        s = lax.dot_general(keys, qa[which], (((1,), (1,)), ((), ())), preferred_element_type=jnp.float32)
        score[...] = s
        best[...] = jnp.max(s, axis=0, keepdims=True)

    def diagonal(i, j, score, best):
        which, g = step_of(i)

        @pl.when((i < STEPS) & (g == 0) & (j + 1 == units_of(which, g)))
        def _():
            late = jnp.where(which == 0, y_lo, 1 - y_lo)
            own_x = jnp.where(which == 0, x, 3 - x)
            row = lax.broadcasted_iota(jnp.int32, (KEYS, WIDE), 0) + (j % 2) * KEYS
            key_pos = ((j // 2) * 32 + (row // 128) * 8 + z) * ROWS + ((row // 64) % 2) * 128 + y_lo * 64 + row % 64
            query_pos = (late * 32 + own_x * 8 + z) * ROWS + lax.broadcasted_iota(jnp.int32, (KEYS, WIDE), 1) % ROWS
            s = jnp.where(key_pos <= query_pos, score[...], HIDE)
            score[...] = s
            best[...] = jnp.max(s, axis=0, keepdims=True)

    def soften(i, j, score, best):
        which, group, late, row = locate(i, j)
        old = top[which]
        new = jnp.maximum(old, best[...])
        weights = jnp.exp2((score[...] - new) * SCALE)
        factor = jnp.exp2((old - new) * SCALE)
        top[which] = new
        total[which] = total[which] * factor + jnp.sum(weights, axis=0, keepdims=True)
        values = kv[1, group, late, pl.ds(row, KEYS), :]
        mixed = lax.dot_general(
            values, weights.astype(jnp.bfloat16), (((0,), (0,)), ((), ())), preferred_element_type=jnp.float32
        )
        acc[which] = acc[which] * factor + mixed

    def hand_back(i, j):
        which, g = step_of(i)

        @pl.when((i < STEPS) & (which == 1) & (g == GROUPS - 1) & (j + 1 == units_of(which, g)))
        def _():
            o_out[...] = (acc[1] / total[1]).astype(jnp.bfloat16)
            s_out[0:1, :] = top[1]
            s_out[1:2, :] = total[1]
            pair_o.start()
            pair_s.start()

    def two_units(turn, state):
        i, j, got = state
        i_b, j_b = advance(i, j)
        got = prepare(i_b, j_b, got)
        scores_of(i_b, j_b, score_b, best_b)
        soften(i, j, score_a, best_a)
        diagonal(i_b, j_b, score_b, best_b)
        hand_back(i, j)
        i_c, j_c = advance(i_b, j_b)
        got = prepare(i_c, j_c, got)
        scores_of(i_c, j_c, score_a, best_a)
        soften(i_b, j_b, score_b, best_b)
        diagonal(i_c, j_c, score_a, best_a)
        hand_back(i_b, j_b)
        return i_c, j_c, got

    units = jnp.int32(0)
    for which in range(2):
        for g in range(GROUPS):
            units = units + units_of(jnp.int32(which), jnp.int32(g))
    scores_of(zero, zero, score_a, best_a)
    diagonal(zero, zero, score_a, best_a)
    lax.fori_loop(0, (units + 1) // 2, two_units, (zero, zero, jnp.int32(1)))

    pair_o.wait_recv()
    pair_s.wait_recv()
    peak = jnp.maximum(top[0], s_in[0:1, :])
    mine = jnp.exp2((top[0] - peak) * SCALE)
    other = jnp.exp2((s_in[0:1, :] - peak) * SCALE) * s_in[1:2, :]
    whole = mine * total[0] + other
    mine, other = mine / whole, other / whole
    for h in range(HEADS):
        part = slice(h * ROWS, (h + 1) * ROWS)
        merged = acc[0, :, part] * mine[:, part] + o_in[:, part].astype(jnp.float32) * other[:, part]
        o_ref[:, h * 128 : (h + 1) * 128] = merged.T.astype(jnp.bfloat16)

    for kind in range(2):
        for turn in range(2):
            away = (core + 2 * turn != y) | (core != kind)
            pl.when(away)(lambda kind=kind, turn=turn: y_copy(kind, turn).wait_send())
    for dx in range(1, 4):
        x_copy(zero, dx).wait_send()

    @pl.when(core == 0)
    def _():
        for way in range(2):
            for hop in range(4):
                ring_copy(way, hop).wait_send()

    @pl.when(core == 1)
    def _():
        for dz in range(1, 8):
            vz_copy(dz).wait_send()
        for g in range(1, GROUPS):
            for dx in range(1, 4):
                x_copy(jnp.int32(g), dx).wait_send()

    for g in range(GROUPS):
        core_copy(jnp.int32(g)).wait_send()
    pair_q.wait_send()
    pair_o.wait_send()
    pair_s.wait_send()


def body(queries, key_rows, value_rows, document_lengths):
    sems = pltpu.SemaphoreType.DMA
    vmem = pl.BlockSpec(memory_space=pltpu.VMEM)
    attended = pl.pallas_call(
        kernel,
        out_shape=jax.ShapeDtypeStruct((ROWS, HEADS * 128), jnp.bfloat16),
        in_specs=[pl.BlockSpec(memory_space=pltpu.SMEM), vmem, vmem, vmem],
        out_specs=vmem,
        scratch_shapes=[
            pltpu.VMEM((2, GROUPS, 2, 512, 128), jnp.bfloat16),
            pltpu.VMEM((GROUPS, 2, 512, 128), jnp.bfloat16),
            pltpu.VMEM((2, WIDE, 256), jnp.bfloat16),
            pltpu.VMEM((ROWS, HEADS * 128), jnp.bfloat16),
            pltpu.VMEM((KEYS, WIDE), jnp.float32),
            pltpu.VMEM((KEYS, WIDE), jnp.float32),
            pltpu.VMEM((2, 128, WIDE), jnp.float32),
            pltpu.VMEM((2, 1, WIDE), jnp.float32),
            pltpu.VMEM((2, 1, WIDE), jnp.float32),
            pltpu.VMEM((1, WIDE), jnp.float32),
            pltpu.VMEM((1, WIDE), jnp.float32),
            pltpu.VMEM((128, WIDE), jnp.bfloat16),
            pltpu.VMEM((128, WIDE), jnp.bfloat16),
            pltpu.VMEM((8, WIDE), jnp.float32),
            pltpu.VMEM((8, WIDE), jnp.float32),
            sems((2, 2)), sems((4,)), sems((GROUPS, 4)), sems((GROUPS, 4)), sems((8,)), sems((8,)),
            sems((4,)), sems((4,)), sems((4,)), sems((4,)),
            sems((GROUPS,)), sems((GROUPS,)), sems((3,)), sems((3,)),
        ],
        compiler_params=pltpu.CompilerParams(
            collective_id=0, has_side_effects=True, vmem_limit_bytes=48 * 2**20
        ),
        cost_estimate=pl.CostEstimate(flops=2 * 2 * 9216 * WIDE * 128, bytes_accessed=2**20, transcendentals=9216 * WIDE),
    )(document_lengths, queries[0], key_rows[0], value_rows[0])
    return attended[None]


def solution(mesh):
    in_specs = (
        P(None, "ctx", "head"),
        P(None, ("ctx", "head"), None),
        P(None, ("ctx", "head"), None),
        P(),
    )
    out_specs = P(None, "ctx", "head")
    return jax.shard_map(body, mesh=mesh, in_specs=in_specs, out_specs=out_specs, check_vma=False)
```

time: 1050 us -> 73.7 us (0.07)
  waiting for transfers between devices: 831 us -> 0 us
  matrix products: 161 us -> 0 us
  Pallas kernels: 0 us -> 69.6 us
  other arithmetic: 34.4 us -> 0 us
  between operations: 13.5 us -> 0.01 us
    all_gather x2 -> x0, waiting for transfers between devices: 829 us -> none  [the longest x1 416 us: body(): key_piece = lax.all_gather(key_rows, ('ctx', 'head'), axis=1, tiled=True)]
    dot_general x128 -> x0, matrix products: 161 us -> none  [the longest x64 86.2 us: update(): jnp.einsum('sqhk,skd->sqhd', weights.astype(jnp.bfloat16), value_block, p...]
    pallas_call x0 -> x1, Pallas kernels: none -> 69.6 us  [body(): pl.pallas_call(kernel, out_shape=jax.ShapeDtypeStruct((ROWS, HEADS * 128)...]
    reduce_sum x129 -> x0, other arithmetic: 18.9 us -> none  [the longest x64 13.4 us: update(): running_total = running_total * factor + jnp.sum(weights, axis=3)]
    and x64 -> x0, other arithmetic: 11 us -> none  [one_block(): (key_pos[None, None, :] <= query_pos[None, :, None]) & (key_pos[None, Non...]
  transfers between devices with their start and end apart: 2 -> 0, of which waited for: 2 -> 0; matrix products, arithmetic and copies ran while one was open for 0% -> 0% of each run, Pallas kernels for 0% -> 0%
where the time goes in v1:
time: 73.7 us; the launch traced here: 73.4 us
  Pallas kernels  69.6 us (94%)
  local copies, waits for them, and re-layouts  3.74 us (5%)
    pallas_call x1, Pallas kernels, body(): pl.pallas_call(kernel, out_shape=jax.ShapeDtypeStruct((ROWS, HEADS * 128)...  69.6 us
    unnamed x9, local copies, waits for them, and re-layouts  3.74 us

profile of v1, /device:TPU:1, one launch (start us, length us, event | category | flops | bytes accessed | tf_op | source)
XLA Modules:
  0.0 73.4 jit_solution(1161088258692237464)
XLA Ops:
  0.0 0.0 copy-start.3
  0.0 0.7 copy-done.3
  0.7 0.0 copy-start
  0.7 0.9 %copy-done = bf16[1,256,512]{2,1,0:T(8,128)(2,1)S(1)} copy-done((bf16[1,256,512]{2,1,0:T(8,128)(2,1)S(1)}, bf16[1,256,512]{2,1,0:T(8,128)(2,1)}, u32[]{:S(2)}) %copy-start) | copy-done | bytes 262168
  1.6 0.0 copy-start.1
  1.6 0.7 copy-done.1
  2.3 0.0 copy-start.2
  2.3 0.7 copy-done.2
  3.0 69.6 %shard_map.46 = bf16[256,512]{1,0:T(8,128)(2,1)S(1)} custom-call(s32[1,4]{1,0:T(1,128)S(1)} %copy-done.3, bf16[256,512]{1,0:T(8,128)(2,1)S(1)} %bitcast.5, bf16[64,128]{1,0:T(8,128)(2,1)S(1)} %bitcast.6, bf16[64,128]{1,0:T(8,128)(2,1)S(1)} %bitcast.7), custom_call_target="tpu_custom_call" | custom-call | flops 4831838208 | bytes 1048576 | tf_op jit(solution)/shard_map/pallas_call | solution.py:403
  72.7 0.7 copy.6
Async XLA Ops:
  0.0 0.7 copy-start.3
  0.7 0.9 %copy-start = (bf16[1,256,512]{2,1,0:T(8,128)(2,1)S(1)}, bf16[1,256,512]{2,1,0:T(8,128)(2,1)}, u32[]{:S(2)}) copy-start(bf16[1,256,512]{2,1,0:T(8,128)(2,1)} %param.4) | copy-start | bytes 786436
  1.6 0.7 copy-start.1
  2.3 0.7 copy-start.2

commit v2 on v1

--- a/solution.py
+++ b/solution.py
@@ -17,6 +17,12 @@
 KEYS = 256
 GROUPS = 8
 STEPS = 2 * GROUPS
+ORDERS = (
+    (0, 8, 9, 10, 11, 12, 13, 14, 15, 1, 2, 3, 4, 5, 6, 7),
+    (0, 8, 9, 1, 10, 2, 11, 12, 3, 13, 14, 15, 4, 5, 6, 7),
+)
+FIRST = ((0, (1, 3, 2, 0)), (1, (0, 1, 7, 2, 6, 3, 5, 4)))
+LAST = ()
 
 
 def device_at(y, x, z, core):
@@ -25,9 +31,9 @@
 
 def kernel(
     lengths, q_ref, k_ref, v_ref, o_ref,
-    kv, dk, qa, q2, score_a, score_b, acc, top, total, best_a, best_b, o_out, o_in, s_out, s_in,
-    y_send, y_recv, x_send, x_recv, vz_send, vz_recv, r_send, r_recv, l_send, l_recv,
-    core_send, core_recv, pair_send, pair_recv,
+    kv, dk, qa, q1, q2, score_a, score_b, acc, top, total, best_a, best_b, o_out, o_in, s_out, s_in,
+    k_send, k_recv, v_send, v_recv, x_send, x_recv, r_send, r_recv, l_send, l_recv,
+    core_send, core_recv, pair_send, pair_recv, q_sem,
 ):
     ctx = lax.axis_index("ctx")
     head = lax.axis_index("head")
@@ -35,17 +41,41 @@
     y_hi, core = head // 2, head % 2
     y = y_hi * 2 + y_lo
     sibling = device_at(y, x, z, 1 - core)
-    partner = device_at(y + 1 - 2 * y_lo, 3 - x, z, core)
+    partner_y = (y + 4 + (1 - 2 * y_lo) * (1 - 2 * core)) % 4
+    partner = device_at(partner_y, 3 - x, z, core)
+
+    q_load = pltpu.make_async_copy(q_ref, q1, q_sem)
+    q_load.start()
 
     barrier = pltpu.get_barrier_semaphore()
-    friends = [
-        device_at((y + dy) % 4, x, z, (core + dc) % 2) for dy in range(4) for dc in range(2) if dy + dc > 0
-    ]
-    friends += [device_at(y, (x + dx) % 4, z, core) for dx in range(1, 4)]
-    friends += [device_at(y, x, (z + dz) % 8, core) for dz in range(1, 8)]
-    friends += [partner]
-    for friend in friends:
-        pl.semaphore_signal(barrier, inc=1, device_id=friend, device_id_type=MESH)
+
+    def greet(y_of, x_of, z_of, core_of):
+        pl.semaphore_signal(barrier, inc=1, device_id=device_at(y_of, x_of, z_of, core_of), device_id_type=MESH)
+
+    @pl.when(core == 0)
+    def _():
+        for yy in range(4):
+            for dx in range(4):
+                if dx == 0:
+                    pl.when((yy != y) | (y_lo != core))(lambda yy=yy: greet(jnp.int32(yy), x, z, y_lo))
+                else:
+                    greet(jnp.int32(yy), (x + dx) % 4, z, y_lo)
+        for dz in (1, 7):
+            greet(y, x, (z + dz) % 8, core)
+
+    @pl.when(core == 1)
+    def _():
+        for yy in range(4):
+            for dz in range(8):
+                if dz == 0:
+                    pl.when((yy != y) | (y_lo != core))(lambda yy=yy: greet(jnp.int32(yy), x, z, y_lo))
+                else:
+                    greet(jnp.int32(yy), x, (z + dz) % 8, y_lo)
+        for dx in range(1, 4):
+            greet(y, (x + dx) % 4, z, core)
+
+    greet(y, x, z, 1 - core)
+    greet(partner_y, 3 - x, z, core)
 
     starts, ends, run = [], [], jnp.int32(0)
     for d in range(4):
@@ -80,29 +110,41 @@
         dk[group, late] = jnp.where(show, 1.0, 0.0).astype(jnp.bfloat16)
         return carry
 
-    fill_queries(0, q_ref)
     lax.fori_loop(0, 2 * GROUPS, fill_keys, 0)
     acc[...] = jnp.zeros_like(acc)
     total[...] = jnp.zeros_like(total)
     top[...] = jnp.full_like(top, -1e38)
-    pl.semaphore_wait(barrier, len(friends))
-
-    def y_copy(kind, turn):
+    pl.semaphore_wait(barrier, 28 + core - jnp.where(y_lo == core, 1, 0))
+
+    def own_copy(kind, turn, step):
         rows = kv.at[kind, z, y_lo, pl.ds(x * 128 + y_hi * 64, 64), :]
+        if kind == 0:
+            target = device_at(core + 2 * turn, (x + step) % 4, z, 0)
+            send, recv = k_send.at[turn, step], k_recv.at[0]
+        else:
+            target = device_at(core + 2 * turn, x, (z + step) % 8, 1)
+            send, recv = v_send.at[turn, step], v_recv.at[step]
         return pltpu.make_async_remote_copy(
-            src_ref=(k_ref, v_ref)[kind], dst_ref=rows, send_sem=y_send.at[kind, turn], recv_sem=y_recv.at[y],
-            device_id=device_at(core + 2 * turn, x, z, kind), device_id_type=MESH,
+            src_ref=(k_ref, v_ref)[kind], dst_ref=rows, send_sem=send, recv_sem=recv,
+            device_id=target, device_id_type=MESH,
         )
 
-    def y_stay(kind):
+    def own_stay(kind):
         rows = kv.at[kind, z, y_lo, pl.ds(x * 128 + y_hi * 64, 64), :]
-        return pltpu.make_async_copy((k_ref, v_ref)[kind], rows, y_recv.at[y])
-
-    for kind in range(2):
-        for turn in range(2):
-            here = (core + 2 * turn == y) & (core == kind)
-            pl.when(here)(lambda kind=kind: y_stay(kind).start())
-            pl.when(jnp.logical_not(here))(lambda kind=kind, turn=turn: y_copy(kind, turn).start())
+        return pltpu.make_async_copy((k_ref, v_ref)[kind], rows, (k_recv, v_recv)[kind].at[0])
+
+    def own_each(act, stay, orders):
+        for kind, order in orders:
+            for step in order:
+                for turn in range(2):
+                    if step:
+                        act(kind, turn, step)
+                    else:
+                        here = (core + 2 * turn == y) & (core == kind)
+                        pl.when(here)(lambda kind=kind: stay(kind))
+                        pl.when(jnp.logical_not(here))(lambda kind=kind, turn=turn: act(kind, turn, 0))
+
+    own_each(lambda *a: own_copy(*a).start(), lambda kind: own_stay(kind).start(), FIRST)
 
     pair_q = pltpu.make_async_remote_copy(
         src_ref=q_ref, dst_ref=q2, send_sem=pair_send.at[0], recv_sem=pair_recv.at[0],
@@ -135,26 +177,19 @@
         part = column((x + 4 - dx) % 4, z_of(g))
         pltpu.make_async_copy(part, part, x_recv.at[g, dx]).wait()
 
-    def vz_copy(dz):
-        part = column(x, z)
-        return pltpu.make_async_remote_copy(
-            src_ref=part, dst_ref=part, send_sem=vz_send.at[dz], recv_sem=vz_recv.at[dz],
-            device_id=device_at(y, x, (z + dz) % 8, core), device_id_type=MESH,
-        )
-
-    def ring_copy(way, hop):
+    def ring_copy(way, hop, part):
         at = (z + 8 + jnp.where(way == 0, -hop, hop)) % 8
-        part = kv.at[0, at] if hop < 3 else kv.at[0, at, way]
+        half = kv.at[0, at, part]
         send, recv = ((r_send, r_recv), (l_send, l_recv))[way]
         return pltpu.make_async_remote_copy(
-            src_ref=part, dst_ref=part, send_sem=send.at[hop], recv_sem=recv.at[hop],
+            src_ref=half, dst_ref=half, send_sem=send.at[hop, part], recv_sem=recv.at[hop, part],
             device_id=device_at(y, x, (z + (1, 7)[way]) % 8, core), device_id_type=MESH,
         )
 
-    def ring_wait(way, hop):
+    def ring_wait(way, hop, part):
         at = (z + 8 + jnp.where(way == 0, -hop - 1, hop + 1)) % 8
-        part = kv.at[0, at] if hop < 3 else kv.at[0, at, way]
-        pltpu.make_async_copy(part, part, (r_recv, l_recv)[way].at[hop]).wait()
+        half = kv.at[0, at, part]
+        pltpu.make_async_copy(half, half, (r_recv, l_recv)[way].at[hop, part]).wait()
 
     def core_copy(g):
         part = kv.at[core, z_of(g)]
@@ -170,88 +205,71 @@
     def relay_values(g):
         dz = (z + 8 - z_of(g)) % 8
         part = column(x, z_of(g))
-        pltpu.make_async_copy(part, part, vz_recv.at[dz]).wait()
+        pltpu.make_async_copy(part, part, v_recv.at[dz]).wait()
         for dx in range(1, 4):
             x_copy(g, dx).start()
 
-    def arrive(g):
-        for hop in range(3):
-            for way in range(2):
-
-                @pl.when((core == 0) & (g == 2 * hop + 1 + way))
-                def _():
-                    ring_wait(way, hop)
-                    ring_copy(way, hop + 1).start()
-
-        @pl.when((core == 0) & (g == 7))
+    def relay(groups):
+        @pl.when(core == 1)
         def _():
-            ring_wait(0, 3)
-            ring_wait(1, 3)
+            for g in groups:
+                relay_values(jnp.int32(g))
+
+    def fetch(g):
+        for hop in range(4):
+
+            @pl.when((core == 0) & (g == 2 * hop + 1))
+            def _():
+                for part in range(2):
+                    for way in range(2):
+                        if hop < 3:
+                            ring_wait(way, hop, part)
+                        elif way == part:
+                            ring_wait(way, hop, part)
+                        if hop < 2 or (hop == 2 and way == part):
+                            ring_copy(way, hop + 1, part).start()
+                core_copy(g).start()
+                if hop < 3:
+                    core_copy(g + 1).start()
 
         @pl.when(core == 1)
         def _():
             for dx in range(1, 4):
                 x_wait(g, dx)
-
-        core_copy(g).start()
-
-        @pl.when((core == 1) & (g == 1))
-        def _():
-            relay_values(jnp.int32(3))
-            relay_values(jnp.int32(4))
-
-        @pl.when((core == 1) & (g == 2))
-        def _():
-            relay_values(jnp.int32(5))
-            relay_values(jnp.int32(6))
-
-        @pl.when((core == 1) & (g == 3))
-        def _():
-            relay_values(jnp.int32(7))
-
-        core_wait(g)
+            core_copy(g).start()
+
+        pl.when(g == 1)(lambda: relay((3, 4)))
+        pl.when(g == 2)(lambda: relay((5, 6)))
+        pl.when(g == 3)(lambda: relay((7,)))
 
     zero = jnp.int32(0)
-    for yy in range(4):
-        rows = kv.at[core, z, yy % 2, pl.ds(x * 128 + (yy // 2) * 64, 64), :]
-        pltpu.make_async_copy(k_ref, rows, y_recv.at[yy]).wait()
-    for dx in range(1, 4):
-        x_copy(zero, dx).start()
+    pair_q.start()
+    q_load.wait()
+    fill_queries(0, q1)
+
+    @pl.when(core == 0)
+    def _():
+        whole = kv.at[0, z]
+        pltpu.make_async_copy(whole, whole, k_recv.at[0]).wait()
+        for part in range(2):
+            for way in range(2):
+                ring_copy(way, 0, part).start()
+
+    relay((0, 1, 2))
+    own_each(lambda *a: own_copy(*a).start(), lambda kind: own_stay(kind).start(), LAST)
 
     @pl.when(core == 1)
     def _():
-        for dz in (1, 7, 2, 6, 3, 5, 4):
-            vz_copy(dz).start()
-
-    pair_q.start()
-    for dx in range(1, 4):
-        x_wait(zero, dx)
-
-    @pl.when(core == 0)
-    def _():
-        ring_copy(0, 0).start()
-        ring_copy(1, 0).start()
+        for dx in range(1, 4):
+            x_wait(zero, dx)
 
     core_copy(zero).start()
 
-    @pl.when(core == 1)
-    def _():
-        relay_values(jnp.int32(1))
-        relay_values(jnp.int32(2))
-
-    core_wait(zero)
-
     def step_of(i):
-        even_set = jnp.where((i >= 4) & (i < 12), 1, 0)
-        even_group = jnp.where(i < 4, i, jnp.where(i < 12, i - 4, i - 8))
-        odd_set = jnp.where((i < 2) | (i == 5) | (i == 8) | (i >= 12), 0, 1)
-        odd_group = jnp.where(
-            i < 2, i,
-            jnp.where(i < 5, i - 2, jnp.where(i == 5, 2, jnp.where(i < 8, i - 3, jnp.where(i == 8, 3, jnp.where(i < 12, i - 4, i - 8))))),
-        )
-        which = jnp.where(y_lo == 0, even_set, odd_set)
-        g = jnp.where(y_lo == 0, even_group, odd_group)
-        return which, g
+        code = jnp.int32(ORDERS[1][0])
+        for n in range(STEPS):
+            code = jnp.where(i == n, jnp.where(y_lo == 0, ORDERS[0][n], ORDERS[1][n]), code)
+        return code // GROUPS, code % GROUPS
 
     def units_of(which, g):
         late = jnp.where(which == 0, y_lo, 1 - y_lo)
@@ -278,14 +296,17 @@
         which, g = step_of(i)
         first = (j == 0) & (i < STEPS)
         fresh = first & (g == got)
-        pl.when(fresh)(lambda: arrive(g))
+        pl.when(fresh)(lambda: core_wait(g))
+        got = jnp.where(fresh, got + 1, got)
 
         @pl.when(first & (which == 1) & (g == 0))
         def _():
             pair_q.wait_recv()
             fill_queries(1, q2)
 
-        return jnp.where(fresh, got + 1, got)
+        last = (j == 0) & (i + 1 < STEPS)
+        pl.when(last & (step_of(i + 1)[1] == got))(lambda: fetch(got))
+        return got
 
     def scores_of(i, j, score, best):
         which, group, late, row = locate(i, j)
@@ -353,9 +374,10 @@
     for which in range(2):
         for g in range(GROUPS):
             units = units + units_of(jnp.int32(which), jnp.int32(g))
+    got = prepare(zero, zero, zero)
     scores_of(zero, zero, score_a, best_a)
     diagonal(zero, zero, score_a, best_a)
-    lax.fori_loop(0, (units + 1) // 2, two_units, (zero, zero, jnp.int32(1)))
+    lax.fori_loop(0, (units + 1) // 2, two_units, (zero, zero, got))
 
     pair_o.wait_recv()
     pair_s.wait_recv()
@@ -369,24 +391,19 @@
         merged = acc[0, :, part] * mine[:, part] + o_in[:, part].astype(jnp.float32) * other[:, part]
         o_ref[:, h * 128 : (h + 1) * 128] = merged.T.astype(jnp.bfloat16)
 
-    for kind in range(2):
-        for turn in range(2):
-            away = (core + 2 * turn != y) | (core != kind)
-            pl.when(away)(lambda kind=kind, turn=turn: y_copy(kind, turn).wait_send())
-    for dx in range(1, 4):
-        x_copy(zero, dx).wait_send()
+    own_each(lambda *a: own_copy(*a).wait_send(), lambda kind: None, FIRST + LAST)
 
     @pl.when(core == 0)
     def _():
         for way in range(2):
             for hop in range(4):
-                ring_copy(way, hop).wait_send()
+                for part in range(2):
+                    if hop < 3 or part == way:
+                        ring_copy(way, hop, part).wait_send()
 
     @pl.when(core == 1)
     def _():
-        for dz in range(1, 8):
-            vz_copy(dz).wait_send()
-        for g in range(1, GROUPS):
+        for g in range(GROUPS):
             for dx in range(1, 4):
                 x_copy(jnp.int32(g), dx).wait_send()
 
@@ -403,12 +420,13 @@
     attended = pl.pallas_call(
         kernel,
         out_shape=jax.ShapeDtypeStruct((ROWS, HEADS * 128), jnp.bfloat16),
-        in_specs=[pl.BlockSpec(memory_space=pltpu.SMEM), vmem, vmem, vmem],
+        in_specs=[pl.BlockSpec(memory_space=pltpu.SMEM)] + [pl.BlockSpec(memory_space=pl.ANY)] * 3,
         out_specs=vmem,
         scratch_shapes=[
             pltpu.VMEM((2, GROUPS, 2, 512, 128), jnp.bfloat16),
             pltpu.VMEM((GROUPS, 2, 512, 128), jnp.bfloat16),
             pltpu.VMEM((2, WIDE, 256), jnp.bfloat16),
+            pltpu.VMEM((ROWS, HEADS * 128), jnp.bfloat16),
             pltpu.VMEM((ROWS, HEADS * 128), jnp.bfloat16),
             pltpu.VMEM((KEYS, WIDE), jnp.float32),
             pltpu.VMEM((KEYS, WIDE), jnp.float32),
@@ -421,12 +439,12 @@
             pltpu.VMEM((128, WIDE), jnp.bfloat16),
             pltpu.VMEM((8, WIDE), jnp.float32),
             pltpu.VMEM((8, WIDE), jnp.float32),
-            sems((2, 2)), sems((4,)), sems((GROUPS, 4)), sems((GROUPS, 4)), sems((8,)), sems((8,)),
-            sems((4,)), sems((4,)), sems((4,)), sems((4,)),
-            sems((GROUPS,)), sems((GROUPS,)), sems((3,)), sems((3,)),
+            sems((2, 4)), sems((1,)), sems((2, 8)), sems((8,)), sems((GROUPS, 4)), sems((GROUPS, 4)),
+            sems((4, 2)), sems((4, 2)), sems((4, 2)), sems((4, 2)),
+            sems((GROUPS,)), sems((GROUPS,)), sems((3,)), sems((3,)), sems,
         ],
         compiler_params=pltpu.CompilerParams(
-            collective_id=0, has_side_effects=True, vmem_limit_bytes=48 * 2**20
+            collective_id=0, has_side_effects=True, vmem_limit_bytes=63 * 2**20
         ),
         cost_estimate=pl.CostEstimate(flops=2 * 2 * 9216 * WIDE * 128, bytes_accessed=2**20, transcendentals=9216 * WIDE),
     )(document_lengths, queries[0], key_rows[0], value_rows[0])

time: 73.7 us -> 61.5 us (0.83)
  Pallas kernels: 69.6 us -> 59.7 us
  local copies, waits for them, and re-layouts: 3.74 us -> 1.67 us
    pallas_call x1, Pallas kernels: 69.6 us -> 59.7 us  [body(): pl.pallas_call(kernel, out_shape=jax.ShapeDtypeStruct((ROWS, HEADS * 128)...]
    unnamed x9 -> x1, local copies, waits for them, and re-layouts: 3.74 us -> 1.67 us
where the time goes in v2:
time: 61.5 us; the launch traced here: 61.3 us
  Pallas kernels  59.7 us (97%)
  local copies, waits for them, and re-layouts  1.67 us (3%)
    pallas_call x1, Pallas kernels, body(): pl.pallas_call(kernel, out_shape=jax.ShapeDtypeStruct((ROWS, HEADS * 128)...  59.7 us
    unnamed x1, local copies, waits for them, and re-layouts  1.67 us

profile of v2, /device:TPU:1, one launch (start us, length us, event | category | flops | bytes accessed | tf_op | source)
XLA Modules:
  0.0 61.3 jit_solution(5188684752808830956)
XLA Ops:
  0.0 59.7 %shard_map.46 = bf16[256,512]{1,0:T(8,128)(2,1)} custom-call(s32[1,4]{1,0:T(1,128)} %lengths.1, bf16[256,512]{1,0:T(8,128)(2,1)} %bitcast.5, bf16[64,128]{1,0:T(8,128)(2,1)} %bitcast.6, bf16[64,128]{1,0:T(8,128)(2,1)} %bitcast.7), custom_call_target="tpu_custom_call" | custom-call | flops 4831838208 | bytes 1048576 | tf_op jit(solution)/shard_map/pallas_call | solution.py:420
  59.7 1.7 %copy.6 = bf16[1,256,512]{2,1,0:T(8,128)(2,1)} copy(bf16[1,256,512]{2,1,0:T(8,128)(2,1)} %bitcast.4) | data formatting | bytes 524288

commit v3 on v2

--- a/solution.py
+++ b/solution.py
@@ -21,6 +21,7 @@
     (0, 8, 9, 10, 11, 12, 13, 14, 15, 1, 2, 3, 4, 5, 6, 7),
     (0, 8, 9, 1, 10, 2, 11, 12, 3, 13, 14, 15, 4, 5, 6, 7),
 )
+RELAY_AT = 2
 FIRST = ((0, (1, 3, 2, 0)), (1, (0, 1, 7, 2, 6, 3, 5, 4)))
 LAST = ()
 
@@ -60,7 +61,7 @@
                     pl.when((yy != y) | (y_lo != core))(lambda yy=yy: greet(jnp.int32(yy), x, z, y_lo))
                 else:
                     greet(jnp.int32(yy), (x + dx) % 4, z, y_lo)
-        for dz in (1, 7):
+        for dz in (1, 2, 6, 7):
             greet(y, x, (z + dz) % 8, core)
 
     @pl.when(core == 1)
@@ -114,7 +115,7 @@
     acc[...] = jnp.zeros_like(acc)
     total[...] = jnp.zeros_like(total)
     top[...] = jnp.full_like(top, -1e38)
-    pl.semaphore_wait(barrier, 28 + core - jnp.where(y_lo == core, 1, 0))
+    pl.semaphore_wait(barrier, 30 - core - jnp.where(y_lo == core, 1, 0))
 
     def own_copy(kind, turn, step):
         rows = kv.at[kind, z, y_lo, pl.ds(x * 128 + y_hi * 64, 64), :]
@@ -178,12 +179,14 @@
         pltpu.make_async_copy(part, part, x_recv.at[g, dx]).wait()
 
     def ring_copy(way, hop, part):
-        at = (z + 8 + jnp.where(way == 0, -hop, hop)) % 8
+        back = 0 if hop < 2 else 2
+        far = 1 + hop % 2
+        at = (z + 8 + jnp.where(way == 0, -back, back)) % 8
         half = kv.at[0, at, part]
         send, recv = ((r_send, r_recv), (l_send, l_recv))[way]
         return pltpu.make_async_remote_copy(
             src_ref=half, dst_ref=half, send_sem=send.at[hop, part], recv_sem=recv.at[hop, part],
-            device_id=device_at(y, x, (z + (1, 7)[way]) % 8, core), device_id_type=MESH,
+            device_id=device_at(y, x, (z + (far, 8 - far)[way]) % 8, core), device_id_type=MESH,
         )
 
     def ring_wait(way, hop, part):
@@ -222,12 +225,8 @@
             def _():
                 for part in range(2):
                     for way in range(2):
-                        if hop < 3:
+                        if hop % 2 == 0 or (hop == 3 and way == part):
                             ring_wait(way, hop, part)
-                        elif way == part:
-                            ring_wait(way, hop, part)
-                        if hop < 2 or (hop == 2 and way == part):
-                            ring_copy(way, hop + 1, part).start()
                 core_copy(g).start()
                 if hop < 3:
                     core_copy(g + 1).start()
@@ -237,6 +236,15 @@
             for dx in range(1, 4):
                 x_wait(g, dx)
             core_copy(g).start()
+
+        @pl.when((core == 0) & (g == RELAY_AT))
+        def _():
+            for part in range(2):
+                for way in range(2):
+                    ring_wait(way, 1, part)
+                    ring_copy(way, 2, part).start()
+            for way in range(2):
+                ring_copy(way, 3, way).start()
 
         pl.when(g == 1)(lambda: relay((3, 4)))
         pl.when(g == 2)(lambda: relay((5, 6)))
@@ -251,19 +259,19 @@
     def _():
         whole = kv.at[0, z]
         pltpu.make_async_copy(whole, whole, k_recv.at[0]).wait()
-        for part in range(2):
-            for way in range(2):
-                ring_copy(way, 0, part).start()
+        for hop in range(2):
+            for part in range(2):
+                for way in range(2):
+                    ring_copy(way, hop, part).start()
 
     relay((0, 1, 2))
-    own_each(lambda *a: own_copy(*a).start(), lambda kind: own_stay(kind).start(), LAST)
-
     @pl.when(core == 1)
     def _():
         for dx in range(1, 4):
             x_wait(zero, dx)
 
     core_copy(zero).start()
+    own_each(lambda *a: own_copy(*a).start(), lambda kind: own_stay(kind).start(), LAST)
 
     def step_of(i):
         code = jnp.int32(ORDERS[1][0])
@@ -292,21 +300,30 @@
         more = (j + 1 < units_of(which, g)) & (i < STEPS)
         return jnp.where(more, i, jnp.minimum(i + 1, STEPS)), jnp.where(more, j + 1, 0)
 
+    def touches_first(i):
+        answer = jnp.bool_(False)
+        for parity, order in enumerate(ORDERS):
+            for n in range(STEPS):
+                if order[n] % GROUPS not in [code % GROUPS for code in order[:n]]:
+                    answer = answer | ((i == n) & (y_lo == parity))
+        return answer
+
     def prepare(i, j, got):
         which, g = step_of(i)
         first = (j == 0) & (i < STEPS)
-        fresh = first & (g == got)
-        pl.when(fresh)(lambda: core_wait(g))
-        got = jnp.where(fresh, got + 1, got)
+        pl.when(first & touches_first(i))(lambda: core_wait(g))
 
         @pl.when(first & (which == 1) & (g == 0))
         def _():
             pair_q.wait_recv()
             fill_queries(1, q2)
 
-        last = (j == 0) & (i + 1 < STEPS)
-        pl.when(last & (step_of(i + 1)[1] == got))(lambda: fetch(got))
-        return got
+        last = j + 1 == units_of(which, g)
+        soon = (first & (i + 1 < STEPS) & (step_of(i + 1)[1] == got)) | (
+            last & (i + 2 < STEPS) & (step_of(i + 2)[1] == got)
+        )
+        pl.when(soon)(lambda: fetch(got))
+        return jnp.where(soon, got + 1, got)
 
     def scores_of(i, j, score, best):
         which, group, late, row = locate(i, j)
@@ -374,7 +391,7 @@
     for which in range(2):
         for g in range(GROUPS):
             units = units + units_of(jnp.int32(which), jnp.int32(g))
-    got = prepare(zero, zero, zero)
+    got = prepare(zero, zero, jnp.int32(1))
     scores_of(zero, zero, score_a, best_a)
     diagonal(zero, zero, score_a, best_a)
     lax.fori_loop(0, (units + 1) // 2, two_units, (zero, zero, got))

time: 61.5 us -> 62.7 us (1.020)
  Pallas kernels: 59.7 us -> 61 us
    pallas_call x1, Pallas kernels: 59.7 us -> 61 us  [body(): pl.pallas_call(kernel, out_shape=jax.ShapeDtypeStruct((ROWS, HEADS * 128)...]
where the time goes in v3:
time: 62.7 us; the launch traced here: 62.6 us
  Pallas kernels  61 us (97%)
  local copies, waits for them, and re-layouts  1.67 us (3%)
    pallas_call x1, Pallas kernels, body(): pl.pallas_call(kernel, out_shape=jax.ShapeDtypeStruct((ROWS, HEADS * 128)...  61 us
    unnamed x1, local copies, waits for them, and re-layouts  1.67 us

profile of v3, /device:TPU:1, one launch (start us, length us, event | category | flops | bytes accessed | tf_op | source)
XLA Modules:
  0.0 62.6 jit_solution(14394510856871478983)
XLA Ops:
  0.0 61.0 %shard_map.46 = bf16[256,512]{1,0:T(8,128)(2,1)} custom-call(s32[1,4]{1,0:T(1,128)} %lengths.1, bf16[256,512]{1,0:T(8,128)(2,1)} %bitcast.5, bf16[64,128]{1,0:T(8,128)(2,1)} %bitcast.6, bf16[64,128]{1,0:T(8,128)(2,1)} %bitcast.7), custom_call_target="tpu_custom_call" | custom-call | flops 4831838208 | bytes 1048576 | tf_op jit(solution)/shard_map/pallas_call | solution.py:437
  61.0 1.7 %copy.6 = bf16[1,256,512]{2,1,0:T(8,128)(2,1)} copy(bf16[1,256,512]{2,1,0:T(8,128)(2,1)} %bitcast.4) | data formatting | bytes 524288
